TPU v7x, 256 devices: a whole 4x4x8 slice. The times are simulated.
256 devices in a mesh: tile: 64 (over z, y, core), frame: 4 (over x).
Axes of the slice: x: 4, y: 4, z: 8, core: 2. Of those that a mesh axis runs over, the one named last changes fastest.
Arguments:
- feats: bfloat16 [4, 16384, 256], P('frame', 'tile'), may hold values from -6 to 6
- routes: int32 [4, 64, 64], P('frame'), may hold values from 0 to 63, as said below
- interp: bfloat16 [4, 64, 16384, 128], P('frame', None, 'tile'), may hold values from -0.5 to 0.5
- w_value: bfloat16 [256, 256], replicated, may hold values from -0.375 to 0.375
- w_attn: bfloat16 [256, 64], replicated, may hold values from -48 to 48
- w_out: bfloat16 [256, 256], replicated, may hold values from -0.375 to 0.375
- grad_out: bfloat16 [4, 16384, 256], P('frame', 'tile'), may hold values from -6 to 6
Outputs:
- grad_feats: bfloat16 [4, 16384, 256], P('frame', 'tile')
- grad_w_value: float32 [256, 256], replicated
- grad_w_attn: float32 [256, 64], replicated
- grad_w_out: float32 [256, 256], replicated
Inputs may be any that keep to these rules, and one draw needn't show every extreme that they name: `routes`: within one frame a reader tile names any one owner tile in at most 2 of its 64 columns; in every frame some owner tile is named in exactly 2 columns by every reader tile.
All inputs are finite; a program needn't handle non-finite values.
Results may differ from a plain program's by a relative error of at most 0.022.
Values may be sent and summed in bfloat16 or wider, within the bound.
A program may use at most 128 MiB of HBM per device.

v0:
```python
import math
import jax
import jax.numpy as jnp
from jax import lax
from jax.sharding import PartitionSpec as P

H = 8
L = 2
P_SIZE = 4


def per_device(feats, routes, interp, w_value, w_attn, w_out, grad_out):
    inputs_now = feats[0]
    grads_now = grad_out[0]
    tile_weights = interp[0]
    routes_now = routes[0]
    tile_count = lax.axis_size("tile")
    myself = lax.axis_index("tile")
    row_count = inputs_now.shape[0]
    model_width = inputs_now.shape[1]
    column_count = tile_weights.shape[0]
    cell_count = tile_weights.shape[2]
    head_count = H
    level_count = L
    point_count = P_SIZE
    group_width = level_count * point_count
    head_dim = model_width // head_count
    capacity = max(2, 2 * column_count // tile_count)
    column = jnp.arange(column_count, dtype=jnp.int32)
    head_of = column // group_width
    level_of = column // point_count % level_count
    lookup_index = level_of * head_count + head_of
    my_routes = lax.dynamic_index_in_dim(routes_now, myself, 0, keepdims=False)
    earlier = (my_routes[None, :] == my_routes[:, None]) & (column[None, :] < column[:, None])
    ranking = jnp.sum(earlier.astype(jnp.int32), axis=1)
    slot_index = my_routes * capacity + ranking
    aimed = routes_now == myself
    ordering = jnp.cumsum(aimed.astype(jnp.int32), axis=1) - 1
    slot_range = jnp.arange(capacity, dtype=jnp.int32)
    picked = aimed[:, None, :] & (ordering[:, None, :] == slot_range[None, :, None])
    filled = jnp.any(picked, axis=2)
    chosen = jnp.sum(jnp.where(picked, lookup_index[None, None, :], 0), axis=2)
    values = jnp.dot(inputs_now, w_value, preferred_element_type=jnp.float32).astype(jnp.bfloat16)
    lookup = values.reshape(level_count, cell_count, head_count, head_dim).transpose(0, 2, 3, 1)
    lookup = lookup.reshape(level_count * head_count, head_dim, cell_count)
    empty = jnp.zeros((column_count, head_dim, cell_count), jnp.bfloat16)
    pieces = lax.all_gather(lookup[None], "tile", axis=0, tiled=True)
    owner_count = pieces.shape[0]
    inside = (my_routes >= 0) & (my_routes < owner_count)
    found = pieces[jnp.clip(my_routes, 0, owner_count - 1), lookup_index]
    fetched = jnp.where(inside[:, None, None], found, empty)
    sampled = jnp.einsum("jdc,jqc->jdq", fetched, tile_weights, preferred_element_type=jnp.float32)
    logits = jnp.dot(inputs_now, w_attn, preferred_element_type=jnp.float32)
    attn = jax.nn.softmax(logits.reshape(row_count, head_count, group_width), axis=-1).reshape(
        row_count, column_count
    )
    attn_heads = attn.T.reshape(head_count, group_width, 1, row_count)
    sampled_heads = sampled.reshape(head_count, group_width, head_dim, row_count)
    mixed = (
        jnp.sum(attn_heads * sampled_heads, axis=1)
        .reshape(model_width, row_count)
        .T.astype(jnp.bfloat16)
    )
    grad_mixed = jnp.dot(grads_now, w_out.T, preferred_element_type=jnp.float32)
    grad_mixed_heads = grad_mixed.T.reshape(head_count, 1, head_dim, row_count)
    grad_attn = jnp.sum(grad_mixed_heads * sampled_heads, axis=2).reshape(column_count, row_count).T
    grad_attn = grad_attn.reshape(row_count, head_count, group_width)
    attn_query = attn.reshape(row_count, head_count, group_width)
    inner_term = jnp.sum(attn_query * grad_attn, axis=-1, keepdims=True)
    grad_logits = (
        (attn_query * (grad_attn - inner_term))
        .reshape(row_count, column_count)
        .astype(jnp.bfloat16)
    )
    grad_sampled = (
        (attn_heads * grad_mixed_heads)
        .reshape(column_count, head_dim, row_count)
        .astype(jnp.bfloat16)
    )
    contrib = jnp.einsum(
        "jdq,jqc->jdc", grad_sampled, tile_weights, preferred_element_type=jnp.float32
    )
    outgoing = (
        jnp.zeros((tile_count * capacity, head_dim, cell_count), jnp.float32)
        .at[slot_index]
        .set(contrib)
    )
    returned = lax.all_to_all(
        outgoing.reshape(tile_count, capacity, head_dim, cell_count).astype(jnp.bfloat16),
        "tile",
        split_axis=0,
        concat_axis=0,
        tiled=True,
    ).astype(jnp.float32)
    table_range = jnp.arange(level_count * head_count, dtype=jnp.int32)
    member = (chosen.reshape(-1)[None, :] == table_range[:, None]) & filled.reshape(-1)[None, :]
    grad_lookup = jnp.dot(
        member.astype(jnp.float32),
        returned.reshape(tile_count * capacity, head_dim * cell_count),
        precision=lax.Precision.HIGHEST,
    )
    grad_values = grad_lookup.reshape(level_count, head_count, head_dim, cell_count).transpose(
        0, 3, 1, 2
    )
    grad_values = grad_values.reshape(row_count, model_width).astype(jnp.bfloat16)
    grad_query = jnp.dot(grad_logits, w_attn.T, preferred_element_type=jnp.float32)
    part_attn = jnp.dot(inputs_now.T, grad_logits, preferred_element_type=jnp.float32)
    part_out = jnp.dot(mixed.T, grads_now, preferred_element_type=jnp.float32)
    grad_inputs = grad_query + jnp.dot(grad_values, w_value.T, preferred_element_type=jnp.float32)
    part_value = jnp.dot(inputs_now.T, grad_values, preferred_element_type=jnp.float32)
    totals = lax.psum((part_value, part_attn, part_out), ("tile", "frame"))
    factor = 1.0 / math.sqrt(tile_count * lax.axis_size("frame") * row_count)
    return (
        grad_inputs.astype(jnp.bfloat16)[None],
        totals[0] * factor,
        totals[1] * factor,
        totals[2] * factor,
    )


def solution(mesh):
    in_specs = (
        P("frame", "tile", None),
        P("frame", None, None),
        P("frame", None, "tile", None),
        P(),
        P(),
        P(),
        P("frame", "tile", None),
    )
    out_specs = (P("frame", "tile", None), P(), P(), P())
    return jax.shard_map(
        per_device, mesh=mesh, in_specs=in_specs, out_specs=out_specs, check_vma=False
    )
```

profile of v0, /device:TPU:1, one launch (start us, length us, event | category | flops | bytes accessed | tf_op | source)
XLA Modules:
  0.0 408.1 jit_solution(1071865935539580949)
XLA Ops:
  7.2 0.0 copy-start
  7.2 0.0 all-gather.2.cloned.1.call-start
  7.2 0.8 copy-done
  8.1 1.1 convolution_convert_fusion
  9.2 0.1 copy.28
  9.3 0.7 copy.29
  10.0 0.0 all-gather.2.cloned.1.call-update
  10.0 0.7 compare_and_fusion
  10.7 0.2 convert_reduce_fusion
  10.9 1.0 fusion.13
  11.9 1.2 fusion.25
  13.1 85.5 %all-gather.2.cloned.1.call-done = bf16[64,16,32,128]{3,2,1,0:T(8,128)(2,1)} async-done(((bf16[1,16,32,128]{3,2,1,0:T(8,128)(2,1)}), bf16[64,16,32,128]{3,2,1,0:T(8,128)(2,1)}) %all-gather.2.cloned.1.call-update) | async-done | bytes 8388624 | tf_op jit(solution)/shard_map/all_gather | solution.py:47
  98.7 4.1 %gather_fusion = bf16[64,32,128]{2,1,0:T(8,128)(2,1)S(1)} fusion(bf16[64,16,32,128]{3,2,1,0:T(8,128)(2,1)} %all-gather.2.cloned.1.call-done, s32[64]{0:T(128)S(1)} %get-tuple-element.30), kind=kCustom, calls=%fused_computation | custom fusion | bytes 1049088 | tf_op jit(solution)/shard_map/gather | solution.py:50
  102.8 5.2 %fusion.8 = (bf16[64,32,256]{2,1,0:T(8,128)(2,1)S(1)}, f32[64,256]{1,0:T(8,128)S(1)}, f32[64,32,256]{2,1,0:T(8,128)}) fusion(f32[64,256]{1,0:T(8,128)S(1)} %bitcast.145, f32[8,32,256]{2,1,0:T(8,128)S(1)} %fusion.25, bf16[1,64,256,128]{3,2,1,0:T(8,128)(2,1)} %param.9, bf16[64,32,128]{2,1,0:T(8,128)(2,1)S(1)} %gather_fusion, ...), kind=kOutput, calls=%fused_computation.12 | convolution fusion | flops 136560640 | bytes 8257600 | tf_op jit(solution)/shard_map/jdc,jqc->jdq/dot_general | solution.py:52
  108.0 0.7 fusion.3
  108.7 0.3 broadcast_in_dim.30
  109.0 2.5 scatter_fusion
  111.5 0.0 copy-start.5
  111.5 1.2 convert_element_type.58
  112.7 6.4 %all-to-all-start = ((bf16[64,2,32,128]{3,2,1,0:T(8,128)(2,1)}), bf16[64,2,32,128]{3,2,1,0:T(8,128)(2,1)S(1)}, u32[]{:S(2)}, u32[]{:S(2)}) async-start(bf16[64,2,32,128]{3,2,1,0:T(8,128)(2,1)} %bitcast.26), calls=%async_computation | async-start | bytes 2097152 | tf_op jit(solution)/shard_map/all_to_all | solution.py:88
  119.1 0.0 all-reduce.3.cloned.1.call-start
  119.1 0.0 copy-done.5
  119.2 0.2 reduce_window_sum.11
  119.4 0.1 select_reduce_fusion
  119.5 0.1 copy.30
  119.6 0.1 eq.77
  119.8 0.1 fusion.45
  119.9 0.1 copy.31
  120.0 0.2 and.128
  120.2 0.3 multiply_reduce_fusion
  120.5 0.8 convolution_bitcast_fusion.1
  121.3 1.8 fusion.27
  123.1 24.0 %all-to-all-done = bf16[64,2,32,128]{3,2,1,0:T(8,128)(2,1)S(1)} async-done(((bf16[64,2,32,128]{3,2,1,0:T(8,128)(2,1)}), bf16[64,2,32,128]{3,2,1,0:T(8,128)(2,1)S(1)}, u32[]{:S(2)}, u32[]{:S(2)}) %all-to-all-start) | async-done | bytes 1048608 | tf_op jit(solution)/shard_map/all_to_all | solution.py:88
  147.1 0.5 copy.50
  147.5 0.0 copy-start.6
  147.5 0.0 copy-start.3
  147.5 0.7 copy.32
  148.2 0.4 fusion.11
  148.6 0.2 copy.33
  148.8 0.9 convolution_bitcast_fusion
  149.7 0.0 all-reduce.3.cloned.1.call-update
  149.7 0.2 fusion.19
  150.0 0.9 fusion.10
  150.8 247.0 %all-reduce.3.cloned.1.call-done = (f32[256,256]{0,1:T(8,128)}, f32[256,64]{0,1:T(8,128)}, f32[256,256]{0,1:T(8,128)}) async-done(((f32[256,256]{0,1:T(8,128)}, f32[256,64]{0,1:T(8,128)}, f32[256,256]{0,1:T(8,128)}), (f32[256,256]{0,1:T(8,128)}, f32[256,64]{0,1:T(8,128)}, f32[256,256]{0,1:T(8,128)})) %all-reduce.3.cloned.1.call-update) | async-done | bytes 589840 | tf_op jit(solution)/shard_map/psum | solution.py:111
  397.8 1.1 broadcast_multiply_fusion
  398.9 0.8 copy.35
  399.8 0.8 copy.36
  400.6 0.6 broadcast_multiply_fusion.2
  (14 shorter events, 0.1 us)
Async XLA Ops:
  7.2 0.9 copy-start
  7.2 91.5 %all-gather.2.cloned.1.call-start = ((), (), s32[]{:S(2)}) async-start(), calls=%async_computation.1 | async-start | bytes 8519680 | tf_op jit(solution)/shard_map/all_gather | solution.py:47
  102.8 5.3 %copy-start.1 = (bf16[1,64,256,128]{3,2,1,0:T(8,128)(2,1)S(1)}, bf16[1,64,256,128]{3,2,1,0:T(8,128)(2,1)}, u32[]{:S(2)}) copy-start(bf16[1,64,256,128]{3,2,1,0:T(8,128)(2,1)} %param.9) | copy-start | bytes 12582916
  111.5 7.6 %copy-start.5 = (s32[1,64,64]{2,1,0:T(8,128)S(1)}, s32[1,64,64]{2,1,0:T(8,128)}, u32[]{:S(2)}) copy-start(s32[1,64,64]{2,1,0:T(8,128)} %param.8) | copy-start | bytes 49156
  112.7 7.5 %copy-start.2 = (f32[64,32,256]{2,1,0:T(8,128)S(1)}, f32[64,32,256]{2,1,0:T(8,128)}, u32[]{:S(2)}) copy-start(f32[64,32,256]{2,1,0:T(8,128)} %get-tuple-element.31) | copy-start | bytes 6291460
  112.7 34.4 %all-to-all-start = ((bf16[64,2,32,128]{3,2,1,0:T(8,128)(2,1)}), bf16[64,2,32,128]{3,2,1,0:T(8,128)(2,1)S(1)}, u32[]{:S(2)}, u32[]{:S(2)}) async-start(bf16[64,2,32,128]{3,2,1,0:T(8,128)(2,1)} %bitcast.26), calls=%async_computation | async-start | bytes 2097152 | tf_op jit(solution)/shard_map/all_to_all | solution.py:88
  119.1 278.7 %all-reduce.3.cloned.1.call-start = ((), (), s32[]{:S(2)}) async-start(), calls=%async_computation.2 | async-start | bytes 1179648 | tf_op jit(solution)/shard_map/psum | solution.py:111
  147.5 2.2 copy-start.6
  147.5 2.4 copy-start.3
  397.8 2.8 copy-start.4
Sparse Core Ops, SparseCore 0:
  11.4 87.2 all-gather.1
  149.8 247.9 all-reduce.2
where the time goes:
time: 408 us
  waiting for transfers between devices  357 us (88%)
  between operations  14.3 us (4%)
  matrix products  14.2 us (3%)
  local copies, waits for them, and re-layouts  12 us (3%)
  starting transfers between devices  6.44 us (2%)
  other arithmetic  4.6 us (1%)
    psum x1, waiting for transfers between devices, per_device(): totals = lax.psum((part_value, part_attn, part_out), ('tile', 'frame'))  247 us
    all_gather x1, waiting for transfers between devices, per_device(): pieces = lax.all_gather(lookup[None], 'tile', axis=0, tiled=True)  85.5 us
    all_to_all x1, waiting for transfers between devices, per_device(): lax.all_to_all(outgoing.reshape(tile_count, capacity, head_dim, cell_coun...  24 us
  transfers between devices with their start and end apart: 3, of which 3 were waited for; matrix products, arithmetic and copies ran while one was open for 2% of the time, Pallas kernels for 0%

commit v1 on v0

--- a/solution.py
+++ b/solution.py
@@ -108,7 +108,7 @@
     part_out = jnp.dot(mixed.T, grads_now, preferred_element_type=jnp.float32)
     grad_inputs = grad_query + jnp.dot(grad_values, w_value.T, preferred_element_type=jnp.float32)
     part_value = jnp.dot(inputs_now.T, grad_values, preferred_element_type=jnp.float32)
-    totals = lax.psum((part_value, part_attn, part_out), ("tile", "frame"))
+    totals = lax.psum(lax.psum((part_value, part_attn, part_out), "frame"), "tile")
     factor = 1.0 / math.sqrt(tile_count * lax.axis_size("frame") * row_count)
     return (
         grad_inputs.astype(jnp.bfloat16)[None],

time: 408 us -> 392 us (0.961)
  waiting for transfers between devices: 357 us -> 340 us
    psum x1 -> x2, waiting for transfers between devices: 247 us -> 230 us  [the longest x1 186 us: per_device(): lax.psum(lax.psum((part_value, part_attn, part_out), 'frame'), 'tile')]
  transfers between devices with their start and end apart: 3 -> 4, of which waited for: 3 -> 4; matrix products, arithmetic and copies ran while one was open for 2% -> 2% of each run, Pallas kernels for 0% -> 0%
where the time goes in v1:
time: 392 us; the launch traced here: 391 us
  waiting for transfers between devices  340 us (87%)
  matrix products  14.2 us (4%)
  between operations  14 us (4%)
  local copies, waits for them, and re-layouts  12 us (3%)
  starting transfers between devices  6.48 us (2%)
  other arithmetic  4.6 us (1%)
    psum x1, waiting for transfers between devices, per_device(): lax.psum(lax.psum((part_value, part_attn, part_out), 'frame'), 'tile')  186 us
    all_gather x1, waiting for transfers between devices, per_device(): pieces = lax.all_gather(lookup[None], 'tile', axis=0, tiled=True)  85.5 us
    psum x1, waiting for transfers between devices, per_device(): lax.psum((part_value, part_attn, part_out), 'frame')  44 us
    all_to_all x1, waiting for transfers between devices, per_device(): lax.all_to_all(outgoing.reshape(tile_count, capacity, head_dim, cell_coun...  24 us
  transfers between devices with their start and end apart: 4, of which 4 were waited for; matrix products, arithmetic and copies ran while one was open for 2% of the time, Pallas kernels for 0%

profile of v1, /device:TPU:1, one launch (start us, length us, event | category | flops | bytes accessed | tf_op | source)
XLA Modules:
  0.0 391.2 jit_solution(10676108977402770224)
XLA Ops:
  7.2 0.0 copy-start
  7.2 0.0 all-gather.2.cloned.1.call-start
  7.2 0.8 copy-done
  8.1 1.1 convolution_convert_fusion
  9.2 0.1 copy.28
  9.3 0.7 copy.29
  10.0 0.0 all-gather.2.cloned.1.call-update
  10.0 0.7 compare_and_fusion
  10.7 0.2 convert_reduce_fusion
  10.9 1.0 fusion.13
  11.9 1.2 fusion.25
  13.1 85.5 %all-gather.2.cloned.1.call-done = bf16[64,16,32,128]{3,2,1,0:T(8,128)(2,1)} async-done(((bf16[1,16,32,128]{3,2,1,0:T(8,128)(2,1)}), bf16[64,16,32,128]{3,2,1,0:T(8,128)(2,1)}) %all-gather.2.cloned.1.call-update) | async-done | bytes 8388624 | tf_op jit(solution)/shard_map/all_gather | solution.py:47
  98.7 4.1 %gather_fusion = bf16[64,32,128]{2,1,0:T(8,128)(2,1)S(1)} fusion(bf16[64,16,32,128]{3,2,1,0:T(8,128)(2,1)} %all-gather.2.cloned.1.call-done, s32[64]{0:T(128)S(1)} %get-tuple-element.33), kind=kCustom, calls=%fused_computation | custom fusion | bytes 1049088 | tf_op jit(solution)/shard_map/gather | solution.py:50
  102.8 5.2 %fusion.8 = (bf16[64,32,256]{2,1,0:T(8,128)(2,1)S(1)}, f32[64,256]{1,0:T(8,128)S(1)}, f32[64,32,256]{2,1,0:T(8,128)}) fusion(f32[64,256]{1,0:T(8,128)S(1)} %bitcast.145, f32[8,32,256]{2,1,0:T(8,128)S(1)} %fusion.25, bf16[1,64,256,128]{3,2,1,0:T(8,128)(2,1)} %param.9, bf16[64,32,128]{2,1,0:T(8,128)(2,1)S(1)} %gather_fusion, ...), kind=kOutput, calls=%fused_computation.12 | convolution fusion | flops 136560640 | bytes 8257600 | tf_op jit(solution)/shard_map/jdc,jqc->jdq/dot_general | solution.py:52
  108.0 0.7 fusion.3
  108.7 0.3 broadcast_in_dim.30
  109.0 2.5 scatter_fusion
  111.5 1.2 convert_element_type.58
  112.7 6.4 %all-to-all-start = ((bf16[64,2,32,128]{3,2,1,0:T(8,128)(2,1)}), bf16[64,2,32,128]{3,2,1,0:T(8,128)(2,1)S(1)}, u32[]{:S(2)}, u32[]{:S(2)}) async-start(bf16[64,2,32,128]{3,2,1,0:T(8,128)(2,1)} %bitcast.26), calls=%async_computation | async-start | bytes 2097152 | tf_op jit(solution)/shard_map/all_to_all | solution.py:88
  119.1 0.0 all-reduce.7.cloned.1.call-start
  119.2 0.2 reduce_window_sum.11
  119.4 0.1 select_reduce_fusion
  119.5 0.1 copy.30
  119.6 0.1 eq.77
  119.8 0.1 fusion.45
  119.9 0.1 copy.31
  120.0 0.2 and.128
  120.2 0.3 multiply_reduce_fusion
  120.5 0.8 convolution_bitcast_fusion.1
  121.3 1.8 fusion.27
  123.1 24.0 %all-to-all-done = bf16[64,2,32,128]{3,2,1,0:T(8,128)(2,1)S(1)} async-done(((bf16[64,2,32,128]{3,2,1,0:T(8,128)(2,1)}), bf16[64,2,32,128]{3,2,1,0:T(8,128)(2,1)S(1)}, u32[]{:S(2)}, u32[]{:S(2)}) %all-to-all-start) | async-done | bytes 1048608 | tf_op jit(solution)/shard_map/all_to_all | solution.py:88
  147.1 0.5 copy.50
  147.5 0.7 copy.32
  148.2 0.0 copy-start.6
  148.2 0.4 fusion.11
  148.6 0.2 copy.33
  148.8 0.9 convolution_bitcast_fusion
  149.7 0.0 all-reduce.7.cloned.1.call-update
  149.7 0.0 all-reduce.5.cloned.1.call-start
  149.8 44.0 %all-reduce.7.cloned.1.call-done = (f32[256,256]{0,1:T(8,128)}, f32[256,64]{0,1:T(8,128)}, f32[256,256]{0,1:T(8,128)}) async-done(((f32[256,256]{0,1:T(8,128)}, f32[256,64]{0,1:T(8,128)}, f32[256,256]{0,1:T(8,128)}), (f32[256,256]{0,1:T(8,128)}, f32[256,64]{0,1:T(8,128)}, f32[256,256]{0,1:T(8,128)})) %all-reduce.7.cloned.1.call-update) | async-done | bytes 589840 | tf_op jit(solution)/shard_map/psum | solution.py:111
  193.8 0.0 all-reduce.5.cloned.1.call-update
  193.8 0.2 fusion.19
  194.0 0.9 fusion.10
  194.9 186.4 %all-reduce.5.cloned.1.call-done = (f32[256,256]{0,1:T(8,128)}, f32[256,64]{0,1:T(8,128)}, f32[256,256]{0,1:T(8,128)}) async-done(((f32[256,256]{0,1:T(8,128)}, f32[256,64]{0,1:T(8,128)}, f32[256,256]{0,1:T(8,128)}), (f32[256,256]{0,1:T(8,128)}, f32[256,64]{0,1:T(8,128)}, f32[256,256]{0,1:T(8,128)})) %all-reduce.5.cloned.1.call-update) | async-done | bytes 589840 | tf_op jit(solution)/shard_map/psum | solution.py:111
  381.3 1.1 broadcast_multiply_fusion
  382.4 0.8 copy.35
  383.2 0.8 copy.36
  384.1 0.6 broadcast_multiply_fusion.2
  (17 shorter events, 0.1 us)
Async XLA Ops:
  7.2 0.9 copy-start
  7.2 91.5 %all-gather.2.cloned.1.call-start = ((), (), s32[]{:S(2)}) async-start(), calls=%async_computation.1 | async-start | bytes 8519680 | tf_op jit(solution)/shard_map/all_gather | solution.py:47
  102.8 5.3 %copy-start.1 = (bf16[1,64,256,128]{3,2,1,0:T(8,128)(2,1)S(1)}, bf16[1,64,256,128]{3,2,1,0:T(8,128)(2,1)}, u32[]{:S(2)}) copy-start(bf16[1,64,256,128]{3,2,1,0:T(8,128)(2,1)} %param.9) | copy-start | bytes 12582916
  111.5 7.6 %copy-start.5 = (s32[1,64,64]{2,1,0:T(8,128)S(1)}, s32[1,64,64]{2,1,0:T(8,128)}, u32[]{:S(2)}) copy-start(s32[1,64,64]{2,1,0:T(8,128)} %param.8) | copy-start | bytes 49156
  112.7 7.5 %copy-start.2 = (f32[64,32,256]{2,1,0:T(8,128)S(1)}, f32[64,32,256]{2,1,0:T(8,128)}, u32[]{:S(2)}) copy-start(f32[64,32,256]{2,1,0:T(8,128)} %get-tuple-element.34) | copy-start | bytes 6291460
  112.7 34.4 %all-to-all-start = ((bf16[64,2,32,128]{3,2,1,0:T(8,128)(2,1)}), bf16[64,2,32,128]{3,2,1,0:T(8,128)(2,1)S(1)}, u32[]{:S(2)}, u32[]{:S(2)}) async-start(bf16[64,2,32,128]{3,2,1,0:T(8,128)(2,1)} %bitcast.26), calls=%async_computation | async-start | bytes 2097152 | tf_op jit(solution)/shard_map/all_to_all | solution.py:88
  119.1 74.7 %all-reduce.7.cloned.1.call-start = ((), (), s32[]{:S(2)}) async-start(), calls=%async_computation.3 | async-start | bytes 1179648 | tf_op jit(solution)/shard_map/psum | solution.py:111
  148.2 45.6 %copy-start.6 = (bf16[256,64]{0,1:T(8,128)(2,1)S(1)}, bf16[256,64]{0,1:T(8,128)(2,1)}, u32[]{:S(2)}) copy-start(bf16[256,64]{0,1:T(8,128)(2,1)} %param.11) | copy-start | bytes 98308
  148.2 45.8 %copy-start.3 = (bf16[256,256]{1,0:T(8,128)(2,1)S(1)}, bf16[256,256]{1,0:T(8,128)(2,1)}, u32[]{:S(2)}) copy-start(bf16[256,256]{1,0:T(8,128)(2,1)} %param.10) | copy-start | bytes 393220
  149.7 231.6 %all-reduce.5.cloned.1.call-start = ((), (), s32[]{:S(2)}) async-start(), calls=%async_computation.2 | async-start | bytes 1179648 | tf_op jit(solution)/shard_map/psum | solution.py:111
  381.3 2.8 copy-start.4
Sparse Core Ops, SparseCore 0:
  11.4 87.2 all-gather.1
  149.8 43.8 all-reduce.6
  197.5 183.7 all-reduce.4
